TPU v7x, 32 devices: a whole 2x2x4 slice. The times are simulated.
32 devices in a mesh: inst: 8 (over y, x, core), tp: 4 (over z).
Axes of the slice: x: 2, y: 2, z: 4, core: 2. Of those that a mesh axis runs over, the one named last changes fastest.
Arguments:
- x_steps: bfloat16 [4, 8, 8, 8192], P(None, 'inst'), may hold values from -6 to 6
- w_query: bfloat16 [8192, 4096], P(None, 'tp'), may hold values from -0.0625 to 0.0625
- w_key: bfloat16 [8192, 1024], P(None, 'tp'), may hold values from -0.0625 to 0.0625
- w_value: bfloat16 [8192, 1024], P(None, 'tp'), may hold values from -0.0625 to 0.0625
- w_out: bfloat16 [4096, 8192], P('tp'), may hold values from -1.1953125 to 1.1953125
- k_pool: bfloat16 [8, 64, 64, 1024], P('inst', None, None, 'tp'), may hold values from -600 to 600
- v_pool: bfloat16 [8, 64, 64, 1024], P('inst', None, None, 'tp'), may hold values from -6 to 6
- page_table: int32 [8, 64], P('inst'), may hold values from 0 to 63, each once within a row
- lengths: int32 [8, 8], P('inst'), may hold values from 1 to 508, 2560 in all within a row
- source_instance: int32 [8, 8], replicated, may hold values from 0 to 7, as said below
- source_slot: int32 [8, 8], replicated, may hold values from 0 to 7, as said below
Outputs:
- layer_out: bfloat16 [4, 8, 8, 8192], P(None, 'inst', None, 'tp')
- key_cache: bfloat16 [8, 8, 512, 1024], P('inst', None, None, 'tp')
- value_cache: bfloat16 [8, 8, 512, 1024], P('inst', None, None, 'tp')
Inputs may be any that keep to these rules, and one draw needn't show every extreme that they name: `page_table`: each instance's row is a permutation of its pages; request r owns entries r * 8 to r * 8 + 7 in order of position. Each instance's 8 lengths sum to 2560. source_instance and source_slot form a permutation of all slots; exactly 7 slots of each instance take a request from another instance, the rest keep their own (source is the slot itself); at most one request goes from one instance to another, and this is reached. `source_slot`: see source_instance.
All inputs are finite; a program needn't handle non-finite values.
Results may differ from a plain program's by a relative error of at most 0.0055.
The roundings to bfloat16 on the way count: a program that leaves them out, or rounds other values in their place, can miss the bound.
Values may be sent and summed in bfloat16 or wider, within the bound.
A program may use at most 192 MiB of HBM per device.

v0:
```python
import math

import jax
import jax.numpy as jnp
from jax import lax
from jax.sharding import PartitionSpec as P

HD = 128


rope_base = 500000.0


def rotary(vectors, positions):
    half = vectors.shape[-1] // 2
    freqs = rope_base ** (-(jnp.arange(half, dtype=jnp.float32) * 2.0 / vectors.shape[-1]))
    angles = positions.astype(jnp.float32)[..., None] * freqs
    cosine = jnp.cos(angles)
    sine = jnp.sin(angles)
    first = vectors[..., :half]
    second = vectors[..., half:]
    return jnp.concatenate(
        [first * cosine - second * sine, second * cosine + first * sine], axis=-1
    )


def local_block(key_view, value_view, lengths_now, tokens, weights):
    w_query, w_key, w_value, w_out = weights
    steps_here, requests, width = tokens.shape
    features = key_view.shape[2]
    kv_local = features // HD
    groups = w_query.shape[1] // (kv_local * HD)
    flat = tokens.reshape(steps_here * requests, width)
    query = jnp.dot(flat, w_query, preferred_element_type=jnp.float32).reshape(
        steps_here, requests, kv_local, groups, HD
    )
    fresh_key = jnp.dot(flat, w_key, preferred_element_type=jnp.float32).reshape(
        steps_here, requests, kv_local, HD
    )
    fresh_value = jnp.dot(flat, w_value, preferred_element_type=jnp.float32)
    positions = lengths_now[None, :] + jnp.arange(steps_here, dtype=jnp.int32)[:, None]
    query = rotary(query, positions[:, :, None, None]).astype(jnp.bfloat16)
    fresh_key = (
        rotary(fresh_key, positions[:, :, None])
        .astype(jnp.bfloat16)
        .reshape(steps_here, requests, features)
    )
    fresh_value = fresh_value.astype(jnp.bfloat16).reshape(steps_here, requests, features)
    places = jnp.arange(key_view.shape[1], dtype=jnp.int32)
    for turn in range(steps_here):
        hit = (places[None, :] == positions[turn][:, None])[:, :, None]
        key_view = jnp.where(hit, fresh_key[turn][:, None], key_view)
        value_view = jnp.where(hit, fresh_value[turn][:, None], value_view)
    valid = (places[None, None, :] <= positions[:, :, None])[:, :, None, :]
    head_mixes = []
    for head in range(kv_local):
        keys_head = key_view[:, :, head * HD : (head + 1) * HD]
        values_head = value_view[:, :, head * HD : (head + 1) * HD]
        scores = jnp.einsum(
            "nrgd,rcd->nrgc", query[:, :, head], keys_head, preferred_element_type=jnp.float32
        ) / math.sqrt(HD)
        scores = jnp.where(valid, scores, -jnp.inf)
        top = jnp.max(scores, axis=-1, keepdims=True)
        probs = jnp.exp(scores - top)
        probs = (probs / jnp.sum(probs, axis=-1, keepdims=True)).astype(jnp.bfloat16)
        head_mixes.append(
            jnp.einsum(
                "nrgc,rcd->nrgd", probs, values_head, preferred_element_type=jnp.float32
            ).astype(jnp.bfloat16)
        )
    mixed = jnp.stack(head_mixes, axis=2)
    terms = jnp.dot(
        mixed.reshape(steps_here * requests, -1), w_out, preferred_element_type=jnp.float32
    )
    terms = terms.reshape(steps_here, requests, -1)
    key_rows = jnp.transpose(fresh_key, (1, 0, 2))
    value_rows = jnp.transpose(fresh_value, (1, 0, 2))
    return (key_view, value_view, lengths_now + steps_here, terms, key_rows, value_rows)


def run_phase(key_view, value_view, lengths_now, phase_x, weights):
    key_view, value_view, lengths_now, terms, key_rows, value_rows = local_block(
        key_view, value_view, lengths_now, phase_x, weights
    )
    results = lax.psum_scatter(terms, "tp", scatter_dimension=2, tiled=True).astype(jnp.bfloat16)
    return (key_view, value_view, lengths_now, results, key_rows, value_rows)


def local(
    x_steps,
    w_query,
    w_key,
    w_value,
    w_out,
    k_pool,
    v_pool,
    page_table,
    lengths,
    source_instance,
    source_slot,
):
    weights = (w_query, w_key, w_value, w_out)
    requests = lengths.shape[1]
    features = k_pool.shape[3]
    table = page_table[0].reshape(requests, -1)
    key_view = k_pool[0][table].reshape(requests, -1, features)
    value_view = v_pool[0][table].reshape(requests, -1, features)
    lengths_now = lengths[0]
    steps_x = x_steps[:, 0]
    instances = lax.axis_size("inst")
    myself = lax.axis_index("inst")
    peers = jnp.arange(instances, dtype=jnp.int32)
    matched = (source_instance == myself) & (peers[:, None] != myself)
    own_slot = jnp.sum(jnp.where(matched, source_slot, 0), axis=1)
    incoming = lax.dynamic_index_in_dim(source_instance, myself, 0, keepdims=False)
    arrived = incoming != myself
    key_view, value_view, lengths_now, first_out, key_rows, value_rows = run_phase(
        key_view, value_view, lengths_now, steps_x[:2], weights
    )
    moved_keys, moved_values, moved_lengths = (
        lax.all_to_all(key_view[own_slot], "inst", split_axis=0, concat_axis=0, tiled=True),
        lax.all_to_all(value_view[own_slot], "inst", split_axis=0, concat_axis=0, tiled=True),
        lax.all_to_all(lengths_now[own_slot], "inst", split_axis=0, concat_axis=0, tiled=True),
    )
    came_keys = moved_keys[incoming]
    came_values = moved_values[incoming]
    came_lengths = moved_lengths[incoming]
    key_view = jnp.where(arrived[:, None, None], came_keys, key_view)
    value_view = jnp.where(arrived[:, None, None], came_values, value_view)
    lengths_now = jnp.where(arrived, came_lengths, lengths_now)
    key_view, value_view, lengths_now, second_out, key_rows, value_rows = run_phase(
        key_view, value_view, lengths_now, steps_x[2:], weights
    )
    layer_out = jnp.concatenate([first_out, second_out], axis=0)[:, None]
    key_cache = key_view[None]
    value_cache = value_view[None]
    return (layer_out, key_cache, value_cache)


def solution(mesh):
    in_specs = (
        P(None, "inst", None, None),
        P(None, "tp"),
        P(None, "tp"),
        P(None, "tp"),
        P("tp", None),
        P("inst", None, None, "tp"),
        P("inst", None, None, "tp"),
        P("inst", None),
        P("inst", None),
        P(),
        P(),
    )
    out_specs = (
        P(None, "inst", None, "tp"),
        P("inst", None, None, "tp"),
        P("inst", None, None, "tp"),
    )
    return jax.shard_map(local, mesh=mesh, in_specs=in_specs, out_specs=out_specs, check_vma=False)
```

profile of v0, /device:TPU:0, one launch (start us, length us, event | category | flops | bytes accessed | tf_op | source)
XLA Modules:
  0.0 198.7 jit_solution(6667243372298355486)
XLA Ops:
  7.2 1.0 select_reduce_fusion
  8.2 0.7 broadcast_add_fusion
  8.9 0.6 gather_fusion.2
  9.6 0.7 copy.65
  10.2 5.2 %all-to-all-start = ((s32[8,1,1]{2,1,0:T(1,128)}), s32[8,1,1]{2,1,0:T(1,128)S(1)}, u32[]{:S(2)}, u32[]{:S(2)}) async-start(s32[8,1,1]{2,1,0:T(1,128)} %copy.65), calls=%async_computation.1 | async-start | bytes 8192 | tf_op jit(solution)/shard_map/all_to_all | solution.py:123
  15.4 6.4 %copy.86 = bf16[256,8192]{1,0:T(8,128)(2,1)} copy(bf16[256,8192]{0,1:T(8,128)(2,1)} %bitcast.233) | data formatting | bytes 8388608 | tf_op jit(solution)/shard_map/dot_general | solution.py:37
  21.9 3.5 %fusion.36 = f32[2,8,2,128]{3,1,2,0:T(8,128)S(1)} fusion(bf16[2,128,8192,1]{2,1,0,3:T(8,128)(2,1)} %bitcast.220, bf16[4,1,8,8192]{3,2,0,1:T(8,128)(2,1)S(1)} %bitcast.227), kind=kOutput, calls=%fused_computation.68 | convolution fusion | flops 67108864 | bytes 4472832 | tf_op jit(solution)/shard_map/dot_general | solution.py:37
  25.4 1.2 fusion.40
  26.6 1.0 copy-done.3
  27.6 0.7 convolution_convert_fusion.5
  28.3 0.7 convolution_convert_fusion.4
  28.9 21.4 %copy.87 = bf16[1024,8192]{1,0:T(8,128)(2,1)} copy(bf16[1024,8192]{0,1:T(8,128)(2,1)} %bitcast.226) | data formatting | bytes 33554432 | tf_op jit(solution)/shard_map/dot_general | solution.py:34
  50.3 8.0 %fusion.34 = f32[2,8,2,4,128]{4,1,3,2,0:T(8,128)S(1)} fusion(bf16[2,4,128,8192,1]{3,2,1,0,4:T(8,128)(2,1)} %bitcast.218, bf16[4,1,8,8192]{3,2,0,1:T(8,128)(2,1)S(1)} %bitcast.231), kind=kOutput, calls=%fused_computation.66 | convolution fusion | flops 268435456 | bytes 17104896 | tf_op jit(solution)/shard_map/dot_general | solution.py:34
  58.3 8.1 %fusion.38 = f32[2,8,2,4,128]{4,1,3,2,0:T(8,128)S(1)} fusion(bf16[2,4,128,8192,1]{3,2,1,0,4:T(8,128)(2,1)} %bitcast.219, bf16[4,1,8,8192]{3,2,0,1:T(8,128)(2,1)S(1)} %bitcast.232), kind=kOutput, calls=%fused_computation.70 | convolution fusion | flops 268435456 | bytes 17104896 | tf_op jit(solution)/shard_map/dot_general | solution.py:34
  66.4 0.7 fusion.72
  67.2 0.5 broadcast.493
  67.7 0.7 reduce.4
  68.5 2.0 %gather_fusion = bf16[64,64,256]{2,1,0:T(8,128)(2,1)} fusion(bf16[64,64,256]{2,1,0:T(8,128)(2,1)S(1)} %bitcast.217, s32[1024]{0:T(1024)S(1)} %pad_clamp_fusion.2), kind=kCustom, calls=%fused_computation | custom fusion | bytes 4194560 | tf_op jit(solution)/shard_map/gather | solution.py:107
  70.5 3.6 %gather_fusion.1 = bf16[64,64,256]{2,1,0:T(8,128)(2,1)} fusion(bf16[64,64,256]{2,1,0:T(8,128)(2,1)} %bitcast.234, s32[1024]{0:T(1024)S(1)} %pad_clamp_fusion.2), kind=kCustom, calls=%fused_computation.1 | custom fusion | bytes 4194560 | tf_op jit(solution)/shard_map/gather | solution.py:106
  74.2 0.2 reduce.1
  74.4 0.7 gather_fusion.3
  75.1 0.7 fusion.70
  76.1 4.8 %fusion.12 = (bf16[8,512,256]{2,1,0:T(8,128)(2,1)S(1)}, bf16[8,512,256]{2,1,0:T(8,128)(2,1)}) fusion(pred[8,512]{1,0:T(8,128)(4,1)S(1)} %get-tuple-element.63, pred[8,512]{1,0:T(8,128)(4,1)S(1)} %get-tuple-element.64, bf16[8,256]{1,0:T(8,128)(2,1)S(1)} %get-tuple-element.32, bf16[8,256]{1,0:T(8,128)(2,1)S(1)} %get-tuple-element.31, ...), kind=kLoop, calls=%fused_computation.23 | loop fusion | flops 4194304 | bytes 8413184 | tf_op jit(solution)/shard_map/jit(_where)/select_n | solution.py:52
  80.9 3.6 %gather_fusion.4 = bf16[8,512,256]{2,1,0:T(8,128)(2,1)} fusion(bf16[8,512,256]{2,1,0:T(8,128)(2,1)} %get-tuple-element.36, s32[1024]{0:T(1024)S(1)} %pad_clamp_fusion.1), kind=kCustom, calls=%fused_computation.4 | custom fusion | bytes 4194336 | tf_op jit(solution)/shard_map/gather | solution.py:122
  84.5 4.3 %all-to-all-start.1 = ((bf16[8,512,256]{2,1,0:T(8,128)(2,1)}), bf16[8,512,256]{2,1,0:T(8,128)(2,1)}, u32[]{:S(2)}, u32[]{:S(2)}) async-start(bf16[8,512,256]{2,1,0:T(8,128)(2,1)} %gather_fusion.4), calls=%async_computation.2 | async-start | bytes 4194304 | tf_op jit(solution)/shard_map/all_to_all | solution.py:122
  88.8 0.7 compare_bitcast_fusion
  89.7 2.0 %gather_fusion.6 = bf16[8,512,256]{2,1,0:T(8,128)(2,1)} fusion(bf16[8,512,256]{2,1,0:T(8,128)(2,1)S(1)} %get-tuple-element.35, s32[1024]{0:T(1024)S(1)} %pad_clamp_fusion.1), kind=kCustom, calls=%fused_computation.6 | custom fusion | bytes 4194336 | tf_op jit(solution)/shard_map/gather | solution.py:121
  91.9 0.6 fusion.80
  92.5 1.5 fusion.30
  94.0 0.6 fusion.79
  94.6 1.5 fusion.31
  96.2 19.3 %all-to-all-done.1 = bf16[8,512,256]{2,1,0:T(8,128)(2,1)} async-done(((bf16[8,512,256]{2,1,0:T(8,128)(2,1)}), bf16[8,512,256]{2,1,0:T(8,128)(2,1)}, u32[]{:S(2)}, u32[]{:S(2)}) %all-to-all-start.1) | async-done | bytes 2097184 | tf_op jit(solution)/shard_map/all_to_all | solution.py:122
  115.5 4.4 %all-to-all-start.2 = ((bf16[8,512,256]{2,1,0:T(8,128)(2,1)}), bf16[8,512,256]{2,1,0:T(8,128)(2,1)}, u32[]{:S(2)}, u32[]{:S(2)}) async-start(bf16[8,512,256]{2,1,0:T(8,128)(2,1)} %gather_fusion.6), calls=%async_computation.3 | async-start | bytes 4194304 | tf_op jit(solution)/shard_map/all_to_all | solution.py:121
  120.1 8.9 %fusion.6 = f32[2,8,8192]{2,1,0:T(8,128)} fusion(bf16[2,8,1024]{2,1,0:T(8,128)(2,1)S(1)} %bitcast.235, bf16[1024,8192]{1,0:T(8,128)(2,1)} %param.15), kind=kOutput, calls=%fused_computation.14 | convolution fusion | flops 268435456 | bytes 17334272 | tf_op jit(solution)/shard_map/dot_general | solution.py:72
  129.4 3.6 %gather_fusion.5 = bf16[8,512,256]{2,1,0:T(8,128)(2,1)} fusion(bf16[8,512,256]{2,1,0:T(8,128)(2,1)} %all-to-all-done.1, s32[1024]{0:T(1024)S(1)} %pad_clamp_fusion), kind=kCustom, calls=%fused_computation.5 | custom fusion | bytes 4194336 | tf_op jit(solution)/shard_map/gather | solution.py:126
  133.0 13.5 %all-to-all-done.2 = bf16[8,512,256]{2,1,0:T(8,128)(2,1)} async-done(((bf16[8,512,256]{2,1,0:T(8,128)(2,1)}), bf16[8,512,256]{2,1,0:T(8,128)(2,1)}, u32[]{:S(2)}, u32[]{:S(2)}) %all-to-all-start.2) | async-done | bytes 2097184 | tf_op jit(solution)/shard_map/all_to_all | solution.py:121
  146.5 3.6 %gather_fusion.7 = bf16[8,512,256]{2,1,0:T(8,128)(2,1)} fusion(bf16[8,512,256]{2,1,0:T(8,128)(2,1)} %all-to-all-done.2, s32[1024]{0:T(1024)S(1)} %pad_clamp_fusion), kind=kCustom, calls=%fused_computation.7 | custom fusion | bytes 4194336 | tf_op jit(solution)/shard_map/gather | solution.py:125
  150.1 5.7 %select_select_fusion = (bf16[8,512,256]{2,1,0:T(8,128)(2,1)}, bf16[8,512,256]{2,1,0:T(8,128)(2,1)}) fusion(bf16[8,512,256]{2,1,0:T(8,128)(2,1)} %gather_fusion.7, bf16[8,512,256]{2,1,0:T(8,128)(2,1)S(1)} %get-tuple-element.35, pred[8]{0:T(512)(128)(4,1)S(1)} %compare_bitcast_fusion, pred[8,512]{1,0:T(8,128)(4,1)S(1)} %get-tuple-element.69, ...), kind=kLoop, calls=%fused_computation.26 | loop fusion | flops 6291456 | bytes 12607496 | tf_op jit(solution)/shard_map/jit(_where)/select_n | solution.py:52
  155.8 1.9 fusion.78
  157.7 1.8 fusion.77
  159.5 0.3 fusion.32
  159.8 0.3 fusion.33
  160.2 8.8 %fusion.4 = f32[2,8,8192]{2,1,0:T(8,128)} fusion(bf16[2,8,1024]{2,1,0:T(8,128)(2,1)S(1)} %bitcast.236, bf16[1024,8192]{1,0:T(8,128)(2,1)} %param.15), kind=kOutput, calls=%fused_computation.12 | convolution fusion | flops 268435456 | bytes 17334272 | tf_op jit(solution)/shard_map/dot_general | solution.py:72
  169.1 0.9 convert_element_type.92
  170.0 8.7 %fusion.9 = (bf16[1,8,512,256]{3,2,1,0:T(8,128)(2,1)}, bf16[1,8,512,256]{3,2,1,0:T(8,128)(2,1)}) fusion(bf16[8,512,256]{2,1,0:T(8,128)(2,1)} %gather_fusion.5, bf16[1,8,512,256]{3,2,1,0:T(8,128)(2,1)} %bitcast.223, pred[8]{0:T(512)(128)(4,1)S(1)} %compare_bitcast_fusion, pred[8,512]{1,0:T(8,128)(4,1)S(1)} %get-tuple-element.63, ...), kind=kLoop, calls=%fused_computation.18 | loop fusion | flops 10485760 | bytes 12632072 | tf_op jit(solution)/shard_map/jit(_where)/select_n | solution.py:53
  178.7 11.5 %reduce-scatter.5.cloned.1.call-done = f32[2,8,2048]{2,1,0:T(8,128)} async-done(((f32[2,8,8192]{2,1,0:T(8,128)}), f32[2,8,2048]{2,1,0:T(8,128)}) %reduce-scatter.5.cloned.1.call-update) | async-done | bytes 131088 | tf_op jit(solution)/shard_map/reduce_scatter | solution.py:85
  190.3 0.9 convert_element_type.101
  191.2 0.7 maximum_bitcast_fusion
  (53 shorter events, 1.9 us)
Async XLA Ops:
  7.2 61.4 %copy-start = (bf16[1,64,64,256]{3,2,1,0:T(8,128)(2,1)S(1)}, bf16[1,64,64,256]{3,2,1,0:T(8,128)(2,1)}, u32[]{:S(2)}) copy-start(bf16[1,64,64,256]{3,2,1,0:T(8,128)(2,1)} %param.17) | copy-start | bytes 6291460
  10.2 64.0 %all-to-all-start = ((s32[8,1,1]{2,1,0:T(1,128)}), s32[8,1,1]{2,1,0:T(1,128)S(1)}, u32[]{:S(2)}, u32[]{:S(2)}) async-start(s32[8,1,1]{2,1,0:T(1,128)} %copy.65), calls=%async_computation.1 | async-start | bytes 8192 | tf_op jit(solution)/shard_map/all_to_all | solution.py:123
  15.4 6.5 %copy-start.4 = (bf16[4,1,8,8192]{3,2,1,0:T(8,128)(2,1)S(1)}, bf16[4,1,8,8192]{3,2,1,0:T(8,128)(2,1)}, u32[]{:S(2)}) copy-start(bf16[4,1,8,8192]{3,2,1,0:T(8,128)(2,1)} %param.11) | copy-start | bytes 1572868
  21.9 3.5 %copy-start.2 = (bf16[256,8192]{1,0:T(8,128)(2,1)S(1)}, bf16[256,8192]{1,0:T(8,128)(2,1)}, u32[]{:S(2)}) copy-start(bf16[256,8192]{1,0:T(8,128)(2,1)} %copy.86) | copy-start | bytes 12582916
  25.4 2.2 %copy-start.3 = (bf16[8192,256]{1,0:T(8,128)(2,1)S(1)}, bf16[8192,256]{1,0:T(8,128)(2,1)}, u32[]{:S(2)}) copy-start(bf16[8192,256]{1,0:T(8,128)(2,1)} %param.14) | copy-start | bytes 12582916
  58.3 8.8 %copy-start.6 = (s32[1,8]{1,0:T(1,128)S(1)}, s32[1,8]{1,0:T(1,128)}, u32[]{:S(2)}) copy-start(s32[1,8]{1,0:T(1,128)} %param.19) | copy-start | bytes 100
  58.3 9.3 %copy-start.7 = (s32[1,64]{1,0:T(1,128)S(1)}, s32[1,64]{1,0:T(1,128)}, u32[]{:S(2)}) copy-start(s32[1,64]{1,0:T(1,128)} %param.18) | copy-start | bytes 772
  84.5 31.0 %all-to-all-start.1 = ((bf16[8,512,256]{2,1,0:T(8,128)(2,1)}), bf16[8,512,256]{2,1,0:T(8,128)(2,1)}, u32[]{:S(2)}, u32[]{:S(2)}) async-start(bf16[8,512,256]{2,1,0:T(8,128)(2,1)} %gather_fusion.4), calls=%async_computation.2 | async-start | bytes 4194304 | tf_op jit(solution)/shard_map/all_to_all | solution.py:122
  115.5 31.0 %all-to-all-start.2 = ((bf16[8,512,256]{2,1,0:T(8,128)(2,1)}), bf16[8,512,256]{2,1,0:T(8,128)(2,1)}, u32[]{:S(2)}, u32[]{:S(2)}) async-start(bf16[8,512,256]{2,1,0:T(8,128)(2,1)} %gather_fusion.6), calls=%async_computation.3 | async-start | bytes 4194304 | tf_op jit(solution)/shard_map/all_to_all | solution.py:121
  119.8 49.3 %reduce-scatter.3.cloned.1.call-start = ((), (), s32[]{:S(2)}) async-start(), calls=%async_computation.5 | async-start | bytes 655360 | tf_op jit(solution)/shard_map/reduce_scatter | solution.py:85
  128.9 61.3 %reduce-scatter.5.cloned.1.call-start = ((), (), s32[]{:S(2)}) async-start(), calls=%async_computation.6 | async-start | bytes 655360 | tf_op jit(solution)/shard_map/reduce_scatter | solution.py:85
  155.8 3.7 %copy-start.5 = (bf16[8,512,256]{2,1,0:T(8,128)(2,1)S(1)}, bf16[8,512,256]{2,1,0:T(8,128)(2,1)}, u32[]{:S(2)}) copy-start(bf16[8,512,256]{2,1,0:T(8,128)(2,1)} %get-tuple-element.34) | copy-start | bytes 6291460
  170.0 21.8 %copy-start.1 = (bf16[1,64,64,256]{3,2,1,0:T(8,128)(2,1)S(1)}, bf16[1,64,64,256]{3,2,1,0:T(8,128)(2,1)}, u32[]{:S(2)}) copy-start(bf16[1,64,64,256]{3,2,1,0:T(8,128)(2,1)} %param.17) | copy-start | bytes 6291460
Sparse Core Ops, SparseCore 0:
  129.1 22.8 reduce-scatter.2
  169.2 21.0 reduce-scatter.4
where the time goes:
time: 200 us; the launch traced here: 199 us
  local copies, waits for them, and re-layouts  50.1 us (25%)
  matrix products  48.3 us (24%)
  waiting for transfers between devices  44.4 us (22%)
  other arithmetic  27.5 us (14%)
  between operations  14.3 us (7%)
  starting transfers between devices  14.1 us (7%)
    dot_general x1, local copies, waits for them, and re-layouts, local_block(): jnp.dot(flat, w_query, preferred_element_type=jnp.float32)  21.4 us
    all_to_all x1, waiting for transfers between devices, local(): lax.all_to_all(value_view[own_slot], 'inst', split_axis=0, concat_axis=0,...  19.3 us
    dot_general x2, matrix products, local_block(): jnp.dot(mixed.reshape(steps_here * requests, -1), w_out, preferred_elemen...  17.7 us
    dot_general x2, matrix products, local_block(): jnp.dot(flat, w_query, preferred_element_type=jnp.float32)  16.1 us
    all_to_all x1, waiting for transfers between devices, local(): lax.all_to_all(key_view[own_slot], 'inst', split_axis=0, concat_axis=0, t...  13.5 us
    reduce_scatter x2, waiting for transfers between devices, run_phase(): lax.psum_scatter(terms, 'tp', scatter_dimension=2, tiled=True)  11.6 us
    select_n x2, other arithmetic, local_block(): key_view = jnp.where(hit, fresh_key[turn][:, None], key_view)  10.5 us
    select_n x1, other arithmetic, local_block(): value_view = jnp.where(hit, fresh_value[turn][:, None], value_view)  8.7 us
  transfers between devices with their start and end apart: 5, of which 3 were waited for; matrix products, arithmetic and copies ran while one was open for 55% of the time, Pallas kernels for 0%

commit v1 on v0

v1 whole, which is shorter than its diff:
```python
import functools
import math

import jax
import jax.numpy as jnp
from jax import lax
from jax.experimental import pallas as pl
from jax.experimental.pallas import tpu as pltpu
from jax.sharding import PartitionSpec as P

HD = 128
GROUP = 4
MESH = pl.DeviceIdType.MESH

rope_base = 500000.0
F32 = jnp.float32
BF16 = jnp.bfloat16


def angles_of(positions):
    half = HD // 2
    freqs = rope_base ** (-(jnp.arange(half, dtype=F32) * 2.0 / HD))
    angles = positions.astype(F32)[..., None] * freqs
    cosine = jnp.cos(angles)
    sine = jnp.sin(angles)
    return jnp.concatenate([cosine, cosine], -1), jnp.concatenate([-sine, sine], -1)


def rotate(vectors, cosine, sine):
    return vectors * cosine + pltpu.roll(vectors, HD // 2, 1) * sine


def rounded(value):
    return value.astype(BF16).astype(F32)


def fused(
    n, t, req, page, chunk, tile,
    tab, cos_ref, sin_ref, x_ref, wq, wk, wv, wo, kp, vp,
    layer, staged,
    pool, send, recv, ext, ext_in, view, wq_b, wk_b, wv_b, wo_b, acc,
    q_s, k_s, kr_s, v_s, m1, m2, mix, rs_out, rs_in,
    pool_sem, w_sem, wo_sem, kv_ss, kv_rs, ex_ss, ex_rs, rs_ss, rs_rs, out_sem,
):
    me = lax.axis_index("inst")
    tp = lax.axis_index("tp")
    feats = kp.shape[2]
    heads = wq.shape[1] // HD
    kvs = feats // HD
    pmax = kp.shape[0] // req
    depth = wq.shape[0]
    steps = depth // chunk
    bufs = wq_b.shape[0]
    width = layer.shape[1]
    at_own, at_slot, at_rel, at_len, at_page = 0, n, 2 * n, 2 * n + req, 2 * n + 2 * req

    pools = [pltpu.make_async_copy(src, pool.at[i], pool_sem.at[i]) for i, src in enumerate((kp, vp))]
    for c in pools:
        c.start()

    def weights(i):
        slot = lax.rem(i, bufs)
        rows = pl.ds(pl.multiple_of(i * chunk, chunk), chunk)
        return [
            pltpu.make_async_copy(src.at[rows], dst.at[slot], w_sem.at[j, slot])
            for j, (src, dst) in enumerate(((wq, wq_b), (wk, wk_b), (wv, wv_b)))
        ]

    barrier = pltpu.get_barrier_semaphore()

    @pl.loop(1, n)
    def _(k):
        pl.semaphore_signal(
            barrier, inc=1, device_id=(lax.rem(me + k, n), tp), device_id_type=MESH
        )

    @pl.loop(1, t)
    def _(k):
        pl.semaphore_signal(
            barrier, inc=1, device_id=(me, lax.rem(tp + k, t)), device_id_type=MESH
        )

    for c in pools:
        c.wait()
    for i in range(bufs - 1):
        for c in weights(i):
            c.start()
    pl.semaphore_wait(barrier, n - 1 + t - 1)

    def move(k):
        return pltpu.make_async_remote_copy(
            src_ref=send.at[k], dst_ref=recv.at[k], send_sem=kv_ss.at[k], recv_sem=kv_rs.at[k],
            device_id=(lax.rem(me + k, n), tp), device_id_type=MESH,
        )

    def move_ext(k):
        return pltpu.make_async_remote_copy(
            src_ref=ext.at[k], dst_ref=ext_in.at[k], send_sem=ex_ss.at[k], recv_sem=ex_rs.at[k],
            device_id=(lax.rem(me + k, n), tp), device_id_type=MESH,
        )

    @pl.loop(1, n)
    def _(k):
        slot = tab[at_own + k]
        for c in range(pmax):
            at = tab[at_page + slot * pmax + c]
            for i in range(2):
                send[k, i, c * page : (c + 1) * page, :] = pool[i, at]
        move(k).start()

    own = tab[at_own]
    for c in range(pmax):
        at = tab[at_page + own * pmax + c]
        for i in range(2):
            recv[0, i, c * page : (c + 1) * page, :] = pool[i, at]

    acc[...] = jnp.zeros_like(acc)
    qw = heads * HD

    @pl.loop(0, steps)
    def _(i):
        @pl.when(i + bufs - 1 < steps)
        def _():
            for c in weights(i + bufs - 1):
                c.start()

        for c in weights(i):
            c.wait()
        slot = lax.rem(i, bufs)
        xs = x_ref[:, pl.ds(pl.multiple_of(i * chunk, chunk), chunk)]
        acc[:, :qw] += jnp.dot(xs, wq_b[slot], preferred_element_type=F32)
        acc[:, qw : qw + feats] += jnp.dot(xs, wk_b[slot], preferred_element_type=F32)
        acc[:, qw + feats :] += jnp.dot(xs, wv_b[slot], preferred_element_type=F32)

    load_out = pltpu.make_async_copy(wo, wo_b, wo_sem)
    load_out.start()

    for turn in range(4):
        rows = slice(turn * req, (turn + 1) * req)
        for h in range(heads):
            q_s[(turn * heads + h) * req : (turn * heads + h + 1) * req, :] = acc[rows, h * HD : (h + 1) * HD]
        for h in range(kvs):
            part = acc[rows, qw + h * HD : qw + (h + 1) * HD]
            k_s[(turn * kvs + h) * req : (turn * kvs + h + 1) * req, :] = part
            if turn < 2:
                kr_s[rows, h * HD : (h + 1) * HD] = rounded(rotate(part, cos_ref[rows, :], sin_ref[rows, :]))
    v_s[...] = rounded(acc[:, qw + feats :])

    @pl.loop(0, n)
    def _(k):
        slot = tab[at_own + k]
        for turn in range(2):
            ext[k, turn : turn + 1, :] = kr_s[pl.ds(turn * req + slot, 1), :]
            ext[k, 2 + turn : 3 + turn, :] = v_s[pl.ds(turn * req + slot, 1), :]
            ext[k, 4 + turn : 5 + turn, :HD] = cos_ref[pl.ds((2 + turn) * req + slot, 1), :]
            ext[k, 6 + turn : 7 + turn, :HD] = sin_ref[pl.ds((2 + turn) * req + slot, 1), :]
        ext[k, 8:9, :] = jnp.full((1, feats), tab[at_len + slot], jnp.int32).astype(F32)
        ext[k, 9:16, :] = jnp.zeros((7, feats), F32)

        @pl.when(k > 0)
        def _():
            move_ext(k).start()

    ext_in[0] = ext[0]

    spots = lax.broadcasted_iota(jnp.int32, (page, feats), 0).astype(F32)

    def inserted(block, c, first, fresh):
        block = block.astype(F32)
        for i, row in enumerate(fresh):
            block = jnp.where(spots == first + (i - c * page), row, block)
        return block.astype(BF16)

    row_q = lax.broadcasted_iota(jnp.int32, (2 * heads, HD), 0)
    late_q = row_q >= heads
    kv_q = lax.rem(row_q, heads) // GROUP

    def attend(base, slot, cosines, sines, first, keys, values):
        q = q_s[pl.ds(base * heads * req + slot, 2 * heads, stride=req), :]
        cosine = jnp.where(late_q, cosines[1], cosines[0])
        sine = jnp.where(late_q, sines[1], sines[0])
        q = rotate(q, cosine, sine)
        q = jnp.concatenate([jnp.where(kv_q == h, q, 0.0) for h in range(kvs)], axis=1).astype(BF16)
        scores = lax.dot_general(q, keys, (((1,), (1,)), ((), ())), preferred_element_type=F32)
        scores = scores * (1.0 / math.sqrt(HD))
        place = lax.broadcasted_iota(jnp.int32, scores.shape, 1).astype(F32)
        late = (lax.broadcasted_iota(jnp.int32, scores.shape, 0) >= heads).astype(F32)
        scores = jnp.where(place <= first + late, scores, -jnp.inf)
        probs = jnp.exp(scores - jnp.max(scores, axis=-1, keepdims=True))
        probs = (probs / jnp.sum(probs, axis=-1, keepdims=True)).astype(BF16)
        mixed = jnp.dot(probs, values, preferred_element_type=F32)
        result = mixed[:, :HD]
        for h in range(1, kvs):
            result = jnp.where(kv_q == h, mixed[:, h * HD : (h + 1) * HD], result)
        return result

    @pl.loop(0, req)
    def _(s):
        first = jnp.full((1, 1), tab[at_len + s], jnp.int32).astype(F32)
        fresh = (
            [kr_s[pl.ds(turn * req + s, 1), :] for turn in range(2)],
            [v_s[pl.ds(turn * req + s, 1), :] for turn in range(2)],
        )
        for c in range(pmax):
            at = tab[at_page + s * pmax + c]
            for i in range(2):
                view[i, c * page : (c + 1) * page, :] = inserted(pool[i, at], c, first, fresh[i])
        cosines = [cos_ref[pl.ds(turn * req + s, 1), :] for turn in range(2)]
        sines = [sin_ref[pl.ds(turn * req + s, 1), :] for turn in range(2)]
        m1[pl.ds(s, 2 * heads, stride=req), :] = attend(0, s, cosines, sines, first, view[0], view[1])

    def sums(phase, k):
        return pltpu.make_async_remote_copy(
            src_ref=rs_out.at[phase, k], dst_ref=rs_in.at[phase, k],
            send_sem=rs_ss.at[phase, k], recv_sem=rs_rs.at[phase, k],
            device_id=(me, lax.rem(tp + k, t)), device_id_type=MESH,
        )

    def project(phase):
        for turn in range(2):
            m = jnp.concatenate(
                [m1[(turn * heads + h) * req : (turn * heads + h + 1) * req, :] for h in range(heads)], axis=1
            )
            mix[turn * req : (turn + 1) * req, :] = m
        lhs = mix[...].astype(BF16)

        @pl.loop(1, t + 1)
        def _(kk):
            k = lax.rem(kk, t)
            target = lax.rem(tp + k, t)

            for c in range(width // tile):
                cols = pl.ds(pl.multiple_of(target * width + c * tile, tile), tile)
                rs_out[phase, k, :, c * tile : (c + 1) * tile] = jnp.dot(
                    lhs, wo_b[:, cols], preferred_element_type=F32
                )

            @pl.when(k > 0)
            def _():
                sums(phase, k).start()

    def finish(phase):
        @pl.loop(1, t)
        def _(k):
            sums(phase, k).wait_recv()

        total = rs_out[phase, 0]
        for k in range(1, t):
            total = total + rs_in[phase, k]
        layer[phase * 2 * req : (phase + 1) * 2 * req, :] = total.astype(BF16)

    load_out.wait()
    project(0)

    def put(k):
        return pltpu.make_async_copy(recv.at[k], staged.at[k], out_sem.at[k])

    @pl.loop(0, n)
    def _(k):
        @pl.when(k > 0)
        def _():
            move_ext(k).wait_recv()
            move(k).wait_recv()

        slot = tab[at_slot + k]
        first = ext_in[k, 8:9, 0:1]
        cosines = [ext_in[k, 4 + turn : 5 + turn, :HD] for turn in range(2)]
        sines = [ext_in[k, 6 + turn : 7 + turn, :HD] for turn in range(2)]
        late = lax.broadcasted_iota(jnp.int32, (2 * kvs, HD), 0) >= kvs
        keys = k_s[pl.ds(2 * kvs * req + slot, 2 * kvs, stride=req), :]
        keys = rounded(rotate(keys, jnp.where(late, cosines[1], cosines[0]), jnp.where(late, sines[1], sines[0])))
        fresh = (
            [ext_in[k, turn : turn + 1, :] for turn in range(2)]
            + [
                jnp.concatenate([keys[turn * kvs + h : turn * kvs + h + 1, :] for h in range(kvs)], axis=1)
                for turn in range(2)
            ],
            [ext_in[k, 2 + turn : 3 + turn, :] for turn in range(2)]
            + [v_s[pl.ds((2 + turn) * req + slot, 1), :] for turn in range(2)],
        )
        for c in range(pmax):
            rows = slice(c * page, (c + 1) * page)
            for i in range(2):
                recv[k, i, rows, :] = inserted(recv[k, i, rows, :], c, first, fresh[i])
        put(k).start()
        m2[pl.ds(k, 2 * heads, stride=n), :] = attend(
            2, slot, cosines, sines, first + 2.0, recv[k, 0], recv[k, 1]
        )

    for s in range(req):
        m1[pl.ds(s, 2 * heads, stride=req), :] = m2[pl.ds(tab[at_rel + s], 2 * heads, stride=n), :]
    project(1)
    finish(0)
    finish(1)

    @pl.loop(0, n)
    def _(k):
        put(k).wait()

        @pl.when(k > 0)
        def _():
            move(k).wait_send()
            move_ext(k).wait_send()

    @pl.loop(1, t)
    def _(k):
        sums(0, k).wait_send()
        sums(1, k).wait_send()


def place(req, rel, staged, keys, values, sem):
    copies = []
    for s in range(req):
        for i, dst in enumerate((keys, values)):
            copies.append(pltpu.make_async_copy(staged.at[rel[s], i], dst.at[0, s], sem.at[i, s]))
    for c in copies:
        c.start()
    for c in copies:
        c.wait()


def local(
    x_steps, w_query, w_key, w_value, w_out, k_pool, v_pool, page_table, lengths,
    source_instance, source_slot,
):
    n = lax.axis_size("inst")
    t = lax.axis_size("tp")
    me = lax.axis_index("inst")
    turns, _, req, depth = x_steps.shape
    pages, page, feats = k_pool.shape[1:]
    context = pages // req * page
    heads = w_query.shape[1] // HD
    kvs = feats // HD
    width = w_out.shape[1] // t
    own_len = lengths[0]

    peers = jnp.arange(n, dtype=jnp.int32)
    slots = jnp.arange(req, dtype=jnp.int32)
    incoming = lax.dynamic_index_in_dim(source_instance, me, 0, keepdims=False)
    goes_to = lax.rem(peers + me, n)
    comes_from = lax.rem(me - peers + n, n)
    hit = (peers[None, :, None] == goes_to[:, None, None]) & (source_instance == me)[None]
    own = jnp.sum(jnp.where(hit, source_slot[None], 0), axis=(1, 2))
    taken = jnp.sum(jnp.where(incoming[None, :] == comes_from[:, None], slots[None, :], 0), axis=1)
    rel = lax.rem(me - incoming + n, n)
    table = jnp.concatenate([own, taken, rel, own_len, page_table[0]]).astype(jnp.int32)
    positions = own_len[None, :] + jnp.arange(turns, dtype=jnp.int32)[:, None]
    cosine, sine = angles_of(positions.reshape(-1))
    x = x_steps.reshape(turns * req, depth)

    chunk, tile, bufs = 512, 512, 3
    smem = pl.BlockSpec(memory_space=pltpu.SMEM)
    vmem = pl.BlockSpec(memory_space=pltpu.VMEM)
    hbm = pl.BlockSpec(memory_space=pl.ANY)
    dma = pltpu.SemaphoreType.DMA
    layer, staged = pl.pallas_call(
        functools.partial(fused, n, t, req, page, chunk, tile),
        out_shape=(
            jax.ShapeDtypeStruct((turns * req, width), BF16),
            jax.ShapeDtypeStruct((n, 2, context, feats), BF16),
        ),
        in_specs=[smem, vmem, vmem, vmem] + [hbm] * 6,
        out_specs=(vmem, hbm),
        scratch_shapes=[
            pltpu.VMEM((2, pages, page, feats), BF16),
            pltpu.VMEM((n, 2, context, feats), BF16),
            pltpu.VMEM((n, 2, context, feats), BF16),
            pltpu.VMEM((n, 16, feats), F32),
            pltpu.VMEM((n, 16, feats), F32),
            pltpu.VMEM((2, context, feats), BF16),
            pltpu.VMEM((bufs, chunk, heads * HD), BF16),
            pltpu.VMEM((bufs, chunk, feats), BF16),
            pltpu.VMEM((bufs, chunk, feats), BF16),
            pltpu.VMEM(w_out.shape, BF16),
            pltpu.VMEM((turns * req, heads * HD + 2 * feats), F32),
            pltpu.VMEM((turns * heads * req, HD), F32),
            pltpu.VMEM((turns * kvs * req, HD), F32),
            pltpu.VMEM((2 * req, feats), F32),
            pltpu.VMEM((turns * req, feats), F32),
            pltpu.VMEM((2 * heads * req, HD), F32),
            pltpu.VMEM((2 * heads * n, HD), F32),
            pltpu.VMEM((2 * req, heads * HD), F32),
            pltpu.VMEM((2, t, 2 * req, width), F32),
            pltpu.VMEM((2, t, 2 * req, width), F32),
            dma((2,)), dma((3, bufs)), dma,
            dma((n,)), dma((n,)), dma((n,)), dma((n,)),
            dma((2, t)), dma((2, t)), dma((n,)),
        ],
        compiler_params=pltpu.CompilerParams(
            collective_id=0, has_side_effects=True, vmem_limit_bytes=56 * 1024 * 1024
        ),
        name="decode",
    )(
        table, cosine, sine, x, w_query, w_key, w_value, w_out,
        k_pool.reshape(pages, page, feats), v_pool.reshape(pages, page, feats),
    )
    key_cache, value_cache = pl.pallas_call(
        functools.partial(place, req),
        out_shape=(jax.ShapeDtypeStruct((1, req, context, feats), BF16),) * 2,
        in_specs=[smem, hbm],
        out_specs=(hbm, hbm),
        scratch_shapes=[dma((2, req))],
        name="place",
    )(rel, staged)
    return layer.reshape(turns, 1, req, width), key_cache, value_cache


def solution(mesh):
    in_specs = (
        P(None, "inst", None, None),
        P(None, "tp"),
        P(None, "tp"),
        P(None, "tp"),
        P("tp", None),
        P("inst", None, None, "tp"),
        P("inst", None, None, "tp"),
        P("inst", None),
        P("inst", None),
        P(),
        P(),
    )
    out_specs = (
        P(None, "inst", None, "tp"),
        P("inst", None, None, "tp"),
        P("inst", None, None, "tp"),
    )
    return jax.shard_map(local, mesh=mesh, in_specs=in_specs, out_specs=out_specs, check_vma=False)
```

time: 200 us -> 209 us (1.045)
  Pallas kernels: 0 us -> 202 us
  matrix products: 48.3 us -> 0 us
  local copies, waits for them, and re-layouts: 50.1 us -> 2.02 us
  waiting for transfers between devices: 44.4 us -> 0 us
  other arithmetic: 27.5 us -> 4.15 us
  starting transfers between devices: 14.1 us -> 0 us
  between operations: 14.3 us -> 0.69 us
    pallas_call x0 -> x2, Pallas kernels: none -> 202 us  [the longest x1 129 us: local(): pl.pallas_call(functools.partial(place, req), out_shape=(jax.ShapeDtypeSt...]
    dot_general x12 -> x0, matrix products: 43.5 us -> none  [the longest x2 17.7 us: local_block(): jnp.dot(mixed.reshape(steps_here * requests, -1), w_out, preferred_elemen...]
    all_to_all x3 -> x0, waiting for transfers between devices: 32.8 us -> none  [the longest x1 19.3 us: local(): lax.all_to_all(value_view[own_slot], 'inst', split_axis=0, concat_axis=0,...]
    dot_general x2 -> x0, local copies, waits for them, and re-layouts: 27.8 us -> none  [the longest x1 21.4 us: local_block(): jnp.dot(flat, w_query, preferred_element_type=jnp.float32)]
    select_n x6 -> x0, other arithmetic: 19.9 us -> none  [the longest x2 10.5 us: local_block(): key_view = jnp.where(hit, fresh_key[turn][:, None], key_view)]
    gather x8 -> x0, local copies, waits for them, and re-layouts: 19.7 us -> none  [the longest x1 3.59 us: local(): key_view = k_pool[0][table].reshape(requests, -1, features)]
    all_to_all x3 -> x0, starting transfers between devices: 13.9 us -> none  [the longest x1 5.17 us: local(): lax.all_to_all(lengths_now[own_slot], 'inst', split_axis=0, concat_axis=0...]
    reduce_scatter x2 -> x0, waiting for transfers between devices: 11.6 us -> none  [run_phase(): lax.psum_scatter(terms, 'tp', scatter_dimension=2, tiled=True)]
  transfers between devices with their start and end apart: 5 -> 0, of which waited for: 3 -> 0; matrix products, arithmetic and copies ran while one was open for 55% -> 0% of each run, Pallas kernels for 0% -> 0%
where the time goes in v1:
time: 209 us
  Pallas kernels  202 us (97%)
  other arithmetic  4.15 us (2%)
    pallas_call x1, Pallas kernels, local(): pl.pallas_call(functools.partial(place, req), out_shape=(jax.ShapeDtypeSt...  129 us
    pallas_call x1, Pallas kernels, local(): pl.pallas_call(functools.partial(fused, n, t, req, page, chunk, tile), ou...  72.7 us

profile of v1, /device:TPU:0, one launch (start us, length us, event | category | flops | bytes accessed | tf_op | source)
XLA Modules:
  0.0 208.7 jit_solution(7998882575143779188)
XLA Ops:
  0.7 0.7 compare_select_fusion
  1.4 0.0 copy-start.1
  1.4 0.2 select_reduce_fusion.1
  1.6 0.8 iota_compare_fusion
  2.3 1.0 select_reduce_fusion
  3.3 1.3 concatenate.9.tab
  4.6 0.7 add_convert_fusion
  5.2 0.1 convert_element_type.11
  5.3 0.1 fusion
  5.5 0.7 pad_maximum_fusion
  6.2 72.7 %decode.1 = (bf16[32,2048]{1,0:T(8,128)(2,1)}, bf16[8,2,512,256]{3,2,1,0:T(8,128)(2,1)}) custom-call(s32[96]{0:T(128)} %concatenate.9.tab, f32[32,128]{1,0:T(8,128)} %get-tuple-element.25.cos_ref, f32[32,128]{1,0:T(8,128)} %get-tuple-element.26.sin_ref, bf16[32,8192]{1,0:T(8,128)(2,1)} %bitcast.13, bf16[8192,1024]{1,0:T(8,128)(2,1)} %wq.1, ...), custom_call_target="tpu_custom_call" | custom-call | tf_op jit(solution)/shard_map/decode/pallas_call | solution.py:356
  78.9 0.0 copy-done.1
  78.9 0.0 copy-start
  78.9 129.1 %place.1 = (bf16[1,8,512,256]{3,2,1,0:T(8,128)(2,1)}, bf16[1,8,512,256]{3,2,1,0:T(8,128)(2,1)}) custom-call(s32[8]{0:T(128)} %copy-done.1, bf16[8,2,512,256]{3,2,1,0:T(8,128)(2,1)} %get-tuple-element.8.staged), custom_call_target="tpu_custom_call" | custom-call | tf_op jit(solution)/shard_map/place/pallas_call | solution.py:397
  208.0 0.0 copy-done
  208.0 0.7 copy.17
  (2 shorter events, 0.0 us)
Async XLA Ops:
  1.4 77.5 %copy-start.1 = (s32[8]{0:T(128)}, s32[8]{0:T(128)S(1)}, u32[]{:S(2)}) copy-start(s32[8]{0:T(128)S(1)} %get-tuple-element.17.rel) | copy-start | bytes 100
  78.9 129.1 %copy-start = (bf16[32,2048]{1,0:T(8,128)(2,1)S(1)}, bf16[32,2048]{1,0:T(8,128)(2,1)}, u32[]{:S(2)}) copy-start(bf16[32,2048]{1,0:T(8,128)(2,1)} %get-tuple-element.7) | copy-start | bytes 393220

commit v2 on v1

--- a/solution.py
+++ b/solution.py
@@ -17,15 +17,6 @@
 BF16 = jnp.bfloat16
 
 
-def angles_of(positions):
-    half = HD // 2
-    freqs = rope_base ** (-(jnp.arange(half, dtype=F32) * 2.0 / HD))
-    angles = positions.astype(F32)[..., None] * freqs
-    cosine = jnp.cos(angles)
-    sine = jnp.sin(angles)
-    return jnp.concatenate([cosine, cosine], -1), jnp.concatenate([-sine, sine], -1)
-
-
 def rotate(vectors, cosine, sine):
     return vectors * cosine + pltpu.roll(vectors, HD // 2, 1) * sine
 
@@ -36,11 +27,11 @@
 
 def fused(
     n, t, req, page, chunk, tile,
-    tab, cos_ref, sin_ref, x_ref, wq, wk, wv, wo, kp, vp,
-    layer, staged,
-    pool, send, recv, ext, ext_in, view, wq_b, wk_b, wv_b, wo_b, acc,
-    q_s, k_s, kr_s, v_s, m1, m2, mix, rs_out, rs_in,
-    pool_sem, w_sem, wo_sem, kv_ss, kv_rs, ex_ss, ex_rs, rs_ss, rs_rs, out_sem,
+    sources, source_slots, table, lens, x_ref, wq, wk, wv, wo, kp, vp,
+    layer, recv,
+    pool, send, ext, ext_in, view, wq_b, wk_b, wv_b, wo_b, acc,
+    cos_ref, sin_ref, q_s, k_s, kr_s, v_s, m1, m2, mix, rs_out, rs_in, tot,
+    pool_sem, w_sem, wo_sem, kv_ss, kv_rs, ex_ss, ex_rs, rs_ss, rs_rs,
 ):
     me = lax.axis_index("inst")
     tp = lax.axis_index("tp")
@@ -52,7 +43,21 @@
     steps = depth // chunk
     bufs = wq_b.shape[0]
     width = layer.shape[1]
-    at_own, at_slot, at_rel, at_len, at_page = 0, n, 2 * n, 2 * n + req, 2 * n + 2 * req
+    half = n // 2
+
+    def own_slot(k):
+        target = lax.rem(me + k, n)
+        found = jnp.int32(0)
+        for s in range(req):
+            found = jnp.where(sources[target, s] == me, source_slots[target, s], found)
+        return found
+
+    def taken_slot(k):
+        origin = lax.rem(me - k + n, n)
+        found = jnp.int32(0)
+        for s in range(req):
+            found = jnp.where(sources[me, s] == origin, s, found)
+        return found
 
     pools = [pltpu.make_async_copy(src, pool.at[i], pool_sem.at[i]) for i, src in enumerate((kp, vp))]
     for c in pools:
@@ -101,18 +106,28 @@
 
     @pl.loop(1, n)
     def _(k):
-        slot = tab[at_own + k]
+        slot = own_slot(k)
         for c in range(pmax):
-            at = tab[at_page + slot * pmax + c]
+            at = table[0, slot * pmax + c]
             for i in range(2):
                 send[k, i, c * page : (c + 1) * page, :] = pool[i, at]
         move(k).start()
 
-    own = tab[at_own]
+    own = own_slot(0)
     for c in range(pmax):
-        at = tab[at_page + own * pmax + c]
+        at = table[0, own * pmax + c]
         for i in range(2):
             recv[0, i, c * page : (c + 1) * page, :] = pool[i, at]
+
+    row_r = lax.broadcasted_iota(jnp.int32, (4 * req, HD), 0)
+    spot = row_r // req
+    for s in range(req):
+        spot = jnp.where(lax.rem(row_r, req) == s, spot + lens[0, s], spot)
+    lane = lax.rem(lax.broadcasted_iota(jnp.int32, (4 * req, HD), 1), HD // 2)
+    angle = spot.astype(F32) * jnp.exp(lane.astype(F32) * (-2.0 * math.log(rope_base) / HD))
+    cos_ref[...] = jnp.cos(angle)
+    sine = jnp.sin(angle)
+    sin_ref[...] = jnp.where(lax.broadcasted_iota(jnp.int32, sine.shape, 1) < HD // 2, -sine, sine)
 
     acc[...] = jnp.zeros_like(acc)
     qw = heads * HD
@@ -148,13 +163,13 @@
 
     @pl.loop(0, n)
     def _(k):
-        slot = tab[at_own + k]
+        slot = own_slot(k)
         for turn in range(2):
             ext[k, turn : turn + 1, :] = kr_s[pl.ds(turn * req + slot, 1), :]
             ext[k, 2 + turn : 3 + turn, :] = v_s[pl.ds(turn * req + slot, 1), :]
             ext[k, 4 + turn : 5 + turn, :HD] = cos_ref[pl.ds((2 + turn) * req + slot, 1), :]
             ext[k, 6 + turn : 7 + turn, :HD] = sin_ref[pl.ds((2 + turn) * req + slot, 1), :]
-        ext[k, 8:9, :] = jnp.full((1, feats), tab[at_len + slot], jnp.int32).astype(F32)
+        ext[k, 8:9, :] = jnp.full((1, feats), lens[0, slot], jnp.int32).astype(F32)
         ext[k, 9:16, :] = jnp.zeros((7, feats), F32)
 
         @pl.when(k > 0)
@@ -196,13 +211,13 @@
 
     @pl.loop(0, req)
     def _(s):
-        first = jnp.full((1, 1), tab[at_len + s], jnp.int32).astype(F32)
+        first = jnp.full((1, 1), lens[0, s], jnp.int32).astype(F32)
         fresh = (
             [kr_s[pl.ds(turn * req + s, 1), :] for turn in range(2)],
             [v_s[pl.ds(turn * req + s, 1), :] for turn in range(2)],
         )
         for c in range(pmax):
-            at = tab[at_page + s * pmax + c]
+            at = table[0, s * pmax + c]
             for i in range(2):
                 view[i, c * page : (c + 1) * page, :] = inserted(pool[i, at], c, first, fresh[i])
         cosines = [cos_ref[pl.ds(turn * req + s, 1), :] for turn in range(2)]
@@ -211,18 +226,15 @@
 
     def sums(phase, k):
         return pltpu.make_async_remote_copy(
-            src_ref=rs_out.at[phase, k], dst_ref=rs_in.at[phase, k],
+            src_ref=rs_out.at[phase, k, : 2 * req if phase == 0 else n],
+            dst_ref=rs_in.at[phase, k, : 2 * req if phase == 0 else n],
             send_sem=rs_ss.at[phase, k], recv_sem=rs_rs.at[phase, k],
             device_id=(me, lax.rem(tp + k, t)), device_id_type=MESH,
         )
 
     def project(phase):
-        for turn in range(2):
-            m = jnp.concatenate(
-                [m1[(turn * heads + h) * req : (turn * heads + h + 1) * req, :] for h in range(heads)], axis=1
-            )
-            mix[turn * req : (turn + 1) * req, :] = m
-        lhs = mix[...].astype(BF16)
+        rows = 2 * req if phase == 0 else n
+        lhs = mix[:rows, :].astype(BF16)
 
         @pl.loop(1, t + 1)
         def _(kk):
@@ -231,7 +243,7 @@
 
             for c in range(width // tile):
                 cols = pl.ds(pl.multiple_of(target * width + c * tile, tile), tile)
-                rs_out[phase, k, :, c * tile : (c + 1) * tile] = jnp.dot(
+                rs_out[phase, k, :rows, c * tile : (c + 1) * tile] = jnp.dot(
                     lhs, wo_b[:, cols], preferred_element_type=F32
                 )
 
@@ -239,30 +251,32 @@
             def _():
                 sums(phase, k).start()
 
-    def finish(phase):
+    def total_of(phase):
+        rows = 2 * req if phase == 0 else n
+
         @pl.loop(1, t)
         def _(k):
             sums(phase, k).wait_recv()
 
-        total = rs_out[phase, 0]
+        total = rs_out[phase, 0, :rows, :]
         for k in range(1, t):
-            total = total + rs_in[phase, k]
-        layer[phase * 2 * req : (phase + 1) * 2 * req, :] = total.astype(BF16)
+            total = total + rs_in[phase, k, :rows, :]
+        return total
 
     load_out.wait()
+    for turn in range(2):
+        for h in range(heads):
+            at = (turn * heads + h) * req
+            mix[turn * req : (turn + 1) * req, h * HD : (h + 1) * HD] = m1[at : at + req, :]
     project(0)
 
-    def put(k):
-        return pltpu.make_async_copy(recv.at[k], staged.at[k], out_sem.at[k])
-
-    @pl.loop(0, n)
-    def _(k):
+    def arrival(k):
         @pl.when(k > 0)
         def _():
             move_ext(k).wait_recv()
             move(k).wait_recv()
 
-        slot = tab[at_slot + k]
+        slot = taken_slot(k)
         first = ext_in[k, 8:9, 0:1]
         cosines = [ext_in[k, 4 + turn : 5 + turn, :HD] for turn in range(2)]
         sines = [ext_in[k, 6 + turn : 7 + turn, :HD] for turn in range(2)]
@@ -282,39 +296,50 @@
             rows = slice(c * page, (c + 1) * page)
             for i in range(2):
                 recv[k, i, rows, :] = inserted(recv[k, i, rows, :], c, first, fresh[i])
-        put(k).start()
         m2[pl.ds(k, 2 * heads, stride=n), :] = attend(
             2, slot, cosines, sines, first + 2.0, recv[k, 0], recv[k, 1]
         )
 
-    for s in range(req):
-        m1[pl.ds(s, 2 * heads, stride=req), :] = m2[pl.ds(tab[at_rel + s], 2 * heads, stride=n), :]
-    project(1)
-    finish(0)
-    finish(1)
-
-    @pl.loop(0, n)
-    def _(k):
-        put(k).wait()
-
-        @pl.when(k > 0)
-        def _():
-            move(k).wait_send()
-            move_ext(k).wait_send()
+    def gathered(group):
+        for turn in range(2):
+            for h in range(heads):
+                at = (turn * heads + h) * n + group * half
+                mix[turn * half : (turn + 1) * half, h * HD : (h + 1) * HD] = m2[at : at + half, :]
+        project(1 + group)
+
+    pl.loop(0, half)(arrival)
+    gathered(0)
+    layer[: 2 * req, :] = total_of(0).astype(BF16)
+    pl.loop(half, n)(arrival)
+    gathered(1)
+    for group in range(2):
+        tot[group * n : (group + 1) * n, :] = total_of(1 + group)
+    rows = []
+    for turn in range(2):
+        for s in range(req):
+            k = lax.rem(me - sources[me, s] + n, n)
+            rows.append(tot[pl.ds(k // half * n + turn * half + lax.rem(k, half), 1), :])
+    layer[2 * req :, :] = jnp.concatenate(rows, axis=0).astype(BF16)
+
+    @pl.loop(1, n)
+    def _(k):
+        move(k).wait_send()
+        move_ext(k).wait_send()
 
     @pl.loop(1, t)
     def _(k):
-        sums(0, k).wait_send()
-        sums(1, k).wait_send()
-
-
-def place(req, rel, staged, keys, values, sem):
+        for phase in range(3):
+            sums(phase, k).wait_send()
+
+
+def place(n, req, sources, staged, keys, values, sem):
+    me = lax.axis_index("inst")
     copies = []
     for s in range(req):
+        k = lax.rem(me - sources[me, s] + n, n)
         for i, dst in enumerate((keys, values)):
-            copies.append(pltpu.make_async_copy(staged.at[rel[s], i], dst.at[0, s], sem.at[i, s]))
-    for c in copies:
-        c.start()
+            copies.append(pltpu.make_async_copy(staged.at[k, i], dst.at[0, s], sem.at[i, s]))
+            copies[-1].start()
     for c in copies:
         c.wait()
 
@@ -325,27 +350,12 @@
 ):
     n = lax.axis_size("inst")
     t = lax.axis_size("tp")
-    me = lax.axis_index("inst")
     turns, _, req, depth = x_steps.shape
     pages, page, feats = k_pool.shape[1:]
     context = pages // req * page
     heads = w_query.shape[1] // HD
     kvs = feats // HD
     width = w_out.shape[1] // t
-    own_len = lengths[0]
-
-    peers = jnp.arange(n, dtype=jnp.int32)
-    slots = jnp.arange(req, dtype=jnp.int32)
-    incoming = lax.dynamic_index_in_dim(source_instance, me, 0, keepdims=False)
-    goes_to = lax.rem(peers + me, n)
-    comes_from = lax.rem(me - peers + n, n)
-    hit = (peers[None, :, None] == goes_to[:, None, None]) & (source_instance == me)[None]
-    own = jnp.sum(jnp.where(hit, source_slot[None], 0), axis=(1, 2))
-    taken = jnp.sum(jnp.where(incoming[None, :] == comes_from[:, None], slots[None, :], 0), axis=1)
-    rel = lax.rem(me - incoming + n, n)
-    table = jnp.concatenate([own, taken, rel, own_len, page_table[0]]).astype(jnp.int32)
-    positions = own_len[None, :] + jnp.arange(turns, dtype=jnp.int32)[:, None]
-    cosine, sine = angles_of(positions.reshape(-1))
     x = x_steps.reshape(turns * req, depth)
 
     chunk, tile, bufs = 512, 512, 3
@@ -357,13 +367,12 @@
         functools.partial(fused, n, t, req, page, chunk, tile),
         out_shape=(
             jax.ShapeDtypeStruct((turns * req, width), BF16),
-            jax.ShapeDtypeStruct((n, 2, context, feats), BF16),
+            pltpu.VMEM((n, 2, context, feats), BF16),
         ),
-        in_specs=[smem, vmem, vmem, vmem] + [hbm] * 6,
-        out_specs=(vmem, hbm),
+        in_specs=[smem] * 4 + [vmem] + [hbm] * 6,
+        out_specs=(vmem, vmem),
         scratch_shapes=[
             pltpu.VMEM((2, pages, page, feats), BF16),
-            pltpu.VMEM((n, 2, context, feats), BF16),
             pltpu.VMEM((n, 2, context, feats), BF16),
             pltpu.VMEM((n, 16, feats), F32),
             pltpu.VMEM((n, 16, feats), F32),
@@ -373,6 +382,8 @@
             pltpu.VMEM((bufs, chunk, feats), BF16),
             pltpu.VMEM(w_out.shape, BF16),
             pltpu.VMEM((turns * req, heads * HD + 2 * feats), F32),
+            pltpu.VMEM((turns * req, HD), F32),
+            pltpu.VMEM((turns * req, HD), F32),
             pltpu.VMEM((turns * heads * req, HD), F32),
             pltpu.VMEM((turns * kvs * req, HD), F32),
             pltpu.VMEM((2 * req, feats), F32),
@@ -380,28 +391,30 @@
             pltpu.VMEM((2 * heads * req, HD), F32),
             pltpu.VMEM((2 * heads * n, HD), F32),
             pltpu.VMEM((2 * req, heads * HD), F32),
-            pltpu.VMEM((2, t, 2 * req, width), F32),
-            pltpu.VMEM((2, t, 2 * req, width), F32),
+            pltpu.VMEM((3, t, max(n, 2 * req), width), F32),
+            pltpu.VMEM((3, t, max(n, 2 * req), width), F32),
+            pltpu.VMEM((2 * n, width), F32),
             dma((2,)), dma((3, bufs)), dma,
             dma((n,)), dma((n,)), dma((n,)), dma((n,)),
-            dma((2, t)), dma((2, t)), dma((n,)),
+            dma((3, t)), dma((3, t)),
         ],
         compiler_params=pltpu.CompilerParams(
             collective_id=0, has_side_effects=True, vmem_limit_bytes=56 * 1024 * 1024
         ),
         name="decode",
     )(
-        table, cosine, sine, x, w_query, w_key, w_value, w_out,
+        source_instance, source_slot, page_table, lengths, x, w_query, w_key, w_value, w_out,
         k_pool.reshape(pages, page, feats), v_pool.reshape(pages, page, feats),
     )
     key_cache, value_cache = pl.pallas_call(
-        functools.partial(place, req),
+        functools.partial(place, n, req),
         out_shape=(jax.ShapeDtypeStruct((1, req, context, feats), BF16),) * 2,
         in_specs=[smem, hbm],
         out_specs=(hbm, hbm),
         scratch_shapes=[dma((2, req))],
+        compiler_params=pltpu.CompilerParams(vmem_limit_bytes=56 * 1024 * 1024),
         name="place",
-    )(rel, staged)
+    )(source_instance, pltpu.with_memory_space_constraint(staged, pltpu.VMEM))
     return layer.reshape(turns, 1, req, width), key_cache, value_cache
 
 

time: 209 us -> 75.9 us (0.36)
  Pallas kernels: 202 us -> 74.4 us
  other arithmetic: 4.15 us -> 0 us
    pallas_call x1, Pallas kernels: 129 us -> 3.01 us  [local(): pl.pallas_call(functools.partial(place, n, req), out_shape=(jax.ShapeDtyp...]
where the time goes in v2:
time: 75.9 us; the launch traced here: 75.7 us
  Pallas kernels  74.4 us (98%)
    pallas_call x1, Pallas kernels, local(): pl.pallas_call(functools.partial(fused, n, t, req, page, chunk, tile), ou...  71.4 us
    pallas_call x1, Pallas kernels, local(): pl.pallas_call(functools.partial(place, n, req), out_shape=(jax.ShapeDtyp...  3.01 us

profile of v2, /device:TPU:0, one launch (start us, length us, event | category | flops | bytes accessed | tf_op | source)
XLA Modules:
  0.0 75.7 jit_solution(9641457777372963778)
XLA Ops:
  0.6 71.4 %decode.1 = (bf16[32,2048]{1,0:T(8,128)(2,1)}, bf16[8,2,512,256]{3,2,1,0:T(8,128)(2,1)S(1)}) custom-call(s32[8,8]{1,0:T(8,128)} %sources.3, s32[8,8]{1,0:T(8,128)} %source_slots.1, s32[1,64]{1,0:T(1,128)} %table.1, s32[1,8]{1,0:T(1,128)} %lens.1, bf16[32,8192]{1,0:T(8,128)(2,1)} %bitcast.8, bf16[8192,1024]{1,0:T(8,128)(2,1)} %wq.1, bf16[8192,256]{1,0:T(8,128)(2,1)} %wk.1, ...), custom_call_target="tpu_custom_call" | custom-call | tf_op jit(solution)/shard_map/decode/pallas_call | solution.py:366
  72.0 0.0 copy-start
  72.0 3.0 %place.1 = (bf16[1,8,512,256]{3,2,1,0:T(8,128)(2,1)}, bf16[1,8,512,256]{3,2,1,0:T(8,128)(2,1)}) custom-call(s32[8,8]{1,0:T(8,128)} %sources.3, bf16[8,2,512,256]{3,2,1,0:T(8,128)(2,1)S(1)} %get-tuple-element.8.staged), custom_call_target="tpu_custom_call" | custom-call | tf_op jit(solution)/shard_map/place/pallas_call | solution.py:409
  75.1 0.0 copy-done
  75.1 0.7 copy.16
Async XLA Ops:
  72.0 3.0 %copy-start = (bf16[32,2048]{1,0:T(8,128)(2,1)S(1)}, bf16[32,2048]{1,0:T(8,128)(2,1)}, u32[]{:S(2)}) copy-start(bf16[32,2048]{1,0:T(8,128)(2,1)} %get-tuple-element.7) | copy-start | bytes 393220

commit v3 on v2

--- a/solution.py
+++ b/solution.py
@@ -15,6 +15,14 @@
 rope_base = 500000.0
 F32 = jnp.float32
 BF16 = jnp.bfloat16
+
+
+def offset_of(k, n):
+    return lax.rem(2 * k, n) + k // (n // 2)
+
+
+def move_of(offset, n):
+    return offset // 2 + lax.rem(offset, 2) * (n // 2)
 
 
 def rotate(vectors, cosine, sine):
@@ -46,14 +54,14 @@
     half = n // 2
 
     def own_slot(k):
-        target = lax.rem(me + k, n)
+        target = lax.rem(me + offset_of(k, n), n)
         found = jnp.int32(0)
         for s in range(req):
             found = jnp.where(sources[target, s] == me, source_slots[target, s], found)
         return found
 
     def taken_slot(k):
-        origin = lax.rem(me - k + n, n)
+        origin = lax.rem(me - offset_of(k, n) + n, n)
         found = jnp.int32(0)
         for s in range(req):
             found = jnp.where(sources[me, s] == origin, s, found)
@@ -95,17 +103,16 @@
     def move(k):
         return pltpu.make_async_remote_copy(
             src_ref=send.at[k], dst_ref=recv.at[k], send_sem=kv_ss.at[k], recv_sem=kv_rs.at[k],
-            device_id=(lax.rem(me + k, n), tp), device_id_type=MESH,
+            device_id=(lax.rem(me + offset_of(k, n), n), tp), device_id_type=MESH,
         )
 
     def move_ext(k):
         return pltpu.make_async_remote_copy(
             src_ref=ext.at[k], dst_ref=ext_in.at[k], send_sem=ex_ss.at[k], recv_sem=ex_rs.at[k],
-            device_id=(lax.rem(me + k, n), tp), device_id_type=MESH,
-        )
-
-    @pl.loop(1, n)
-    def _(k):
+            device_id=(lax.rem(me + offset_of(k, n), n), tp), device_id_type=MESH,
+        )
+
+    def depart(k):
         slot = own_slot(k)
         for c in range(pmax):
             at = table[0, slot * pmax + c]
@@ -113,6 +120,7 @@
                 send[k, i, c * page : (c + 1) * page, :] = pool[i, at]
         move(k).start()
 
+    pl.loop(1, half)(depart)
     own = own_slot(0)
     for c in range(pmax):
         at = table[0, own * pmax + c]
@@ -224,6 +232,8 @@
         sines = [sin_ref[pl.ds(turn * req + s, 1), :] for turn in range(2)]
         m1[pl.ds(s, 2 * heads, stride=req), :] = attend(0, s, cosines, sines, first, view[0], view[1])
 
+    pl.loop(half, n)(depart)
+
     def sums(phase, k):
         return pltpu.make_async_remote_copy(
             src_ref=rs_out.at[phase, k, : 2 * req if phase == 0 else n],
@@ -317,7 +327,7 @@
     rows = []
     for turn in range(2):
         for s in range(req):
-            k = lax.rem(me - sources[me, s] + n, n)
+            k = move_of(lax.rem(me - sources[me, s] + n, n), n)
             rows.append(tot[pl.ds(k // half * n + turn * half + lax.rem(k, half), 1), :])
     layer[2 * req :, :] = jnp.concatenate(rows, axis=0).astype(BF16)
 
@@ -336,7 +346,7 @@
     me = lax.axis_index("inst")
     copies = []
     for s in range(req):
-        k = lax.rem(me - sources[me, s] + n, n)
+        k = move_of(lax.rem(me - sources[me, s] + n, n), n)
         for i, dst in enumerate((keys, values)):
             copies.append(pltpu.make_async_copy(staged.at[k, i], dst.at[0, s], sem.at[i, s]))
             copies[-1].start()

time: 75.9 us -> 70.2 us (0.925)
  Pallas kernels: 74.4 us -> 68.7 us
    pallas_call x1, Pallas kernels: 71.4 us -> 65.7 us  [local(): pl.pallas_call(functools.partial(fused, n, t, req, page, chunk, tile), ou...]
where the time goes in v3:
time: 70.2 us; the launch traced here: 70 us
  Pallas kernels  68.7 us (98%)
    pallas_call x1, Pallas kernels, local(): pl.pallas_call(functools.partial(fused, n, t, req, page, chunk, tile), ou...  65.7 us
    pallas_call x1, Pallas kernels, local(): pl.pallas_call(functools.partial(place, n, req), out_shape=(jax.ShapeDtyp...  3.01 us

profile of v3, /device:TPU:0, one launch (start us, length us, event | category | flops | bytes accessed | tf_op | source)
XLA Modules:
  0.0 70.0 jit_solution(10342218204113402470)
XLA Ops:
  0.6 65.7 %decode.1 = (bf16[32,2048]{1,0:T(8,128)(2,1)}, bf16[8,2,512,256]{3,2,1,0:T(8,128)(2,1)S(1)}) custom-call(s32[8,8]{1,0:T(8,128)} %sources.3, s32[8,8]{1,0:T(8,128)} %source_slots.1, s32[1,64]{1,0:T(1,128)} %table.1, s32[1,8]{1,0:T(1,128)} %lens.1, bf16[32,8192]{1,0:T(8,128)(2,1)} %bitcast.8, bf16[8192,1024]{1,0:T(8,128)(2,1)} %wq.1, bf16[8192,256]{1,0:T(8,128)(2,1)} %wk.1, ...), custom_call_target="tpu_custom_call" | custom-call | tf_op jit(solution)/shard_map/decode/pallas_call | solution.py:376
  66.3 0.0 copy-start
  66.3 3.0 %place.1 = (bf16[1,8,512,256]{3,2,1,0:T(8,128)(2,1)}, bf16[1,8,512,256]{3,2,1,0:T(8,128)(2,1)}) custom-call(s32[8,8]{1,0:T(8,128)} %sources.3, bf16[8,2,512,256]{3,2,1,0:T(8,128)(2,1)S(1)} %get-tuple-element.8.staged), custom_call_target="tpu_custom_call" | custom-call | tf_op jit(solution)/shard_map/place/pallas_call | solution.py:419
  69.3 0.0 copy-done
  69.3 0.7 copy.16
Async XLA Ops:
  66.3 3.0 %copy-start = (bf16[32,2048]{1,0:T(8,128)(2,1)S(1)}, bf16[32,2048]{1,0:T(8,128)(2,1)}, u32[]{:S(2)}) copy-start(bf16[32,2048]{1,0:T(8,128)(2,1)} %get-tuple-element.7) | copy-start | bytes 393220
